TPU v7x, 32 devices: a whole 2x2x4 slice. The times are simulated.
32 devices in a mesh: groups: 2 (over x), seq: 8 (over z, y), chan: 2 (over core).
Axes of the slice: x: 2, y: 2, z: 4, core: 2. Of those that a mesh axis runs over, the one named last changes fastest.
Arguments:
- query_feat: bfloat16 [4096, 2048], P('chan', ('groups', 'seq')), parts along dimension 1, may hold values from -6 to 6
- key_feat: bfloat16 [4096, 2048], P('chan', ('groups', 'seq')), parts along dimension 1, may hold values from -6 to 6
- value_feat: bfloat16 [4096, 2048], P('chan', ('groups', 'seq')), parts along dimension 1, may hold values from -6 to 6
- filter_seed: int32 [16], replicated, may hold values from 1 to 511
- filter_in: float32 [32, 64], replicated, may hold values from -1 to 1
- filter_bias: float32 [64], replicated, may hold values from -3.140625 to 3.140625
- filter_out: float32 [64, 256], P(None, 'chan'), may hold values from -0.75 to 0.75
- decay_rate: float32 [256], P('chan'), may hold values from 0.000390625 to 0.0078125
- reach_blocks: int32 [256], P('chan'), may hold values from 1 to 2, as said below
- skip_gain: float32 [4096], P('chan'), may hold values from -4 to 4
- out_weight: bfloat16 [4096, 2048], P('chan'), may hold values from -0.09375 to 0.09375
Outputs:
- projected: bfloat16 [2048, 2048], P(('groups', 'seq'), 'chan'), parts along dimension 0
There are 2 independent parts, one for each index of `groups`. A program takes and returns all parts, laid end to end along the dimension named above; an argument that names none is the same for every part. Nothing has to cross between parts.
Inputs may be any that keep to these rules, and one draw needn't show every extreme that they name: `reach_blocks`: some filter group reaches 2 blocks and some filter group only one.
All inputs are finite; a program needn't handle non-finite values.
Results may differ from a plain program's by a relative error of at most 0.0059.
Values may be sent and summed in bfloat16 or wider, within the bound.
A program may use at most 128 MiB of HBM per device.

v0:
```python
import functools
import math

import jax
import jax.numpy as jnp
from jax import lax
from jax.experimental import pallas as pl
from jax.experimental.pallas import tpu as pltpu
from jax.sharding import PartitionSpec as P

MESH = pl.DeviceIdType.MESH
CHUNK = 256
PIECE = 256
AHEAD = 4
PARTS = 2


def as_column(row, size):
    rows = lax.broadcasted_iota(jnp.int32, (size, size), 0)
    cols = lax.broadcasted_iota(jnp.int32, (size, size), 1)
    spread = jnp.broadcast_to(row, (size, size))
    return jnp.sum(jnp.where(rows == cols, spread, 0.0), axis=1, keepdims=True)


def halo_kernel(
    seq_count,
    query_hbm,
    key_hbm,
    value_hbm,
    seed_hbm,
    in_hbm,
    bias_hbm,
    fout_hbm,
    decay_hbm,
    reach_hbm,
    skip_hbm,
    weight_hbm,
    out_ref,
    seed_ref,
    in_ref,
    bias_ref,
    fout_ref,
    decay_ref,
    reach_ref,
    skip_ref,
    query,
    key,
    value,
    weight,
    product,
    back_two,
    back_one,
    taps,
    skip_wide,
    gated,
    total,
    part_out,
    part_in,
    small_sem,
    key_sem,
    value_sem,
    query_sem,
    weight_sem,
    far_send,
    far_recv,
    near_send,
    near_recv,
    core_send,
    core_recv,
):
    channels, block = product.shape
    filters = taps.shape[0]
    per_group = channels // filters
    lags = taps.shape[1]
    chunks = channels // CHUNK
    pieces = channels // PIECE
    groups_piece = PIECE // per_group
    cols = out_ref.shape[1]
    seq_len = seq_count * block

    me = lax.axis_index("seq")
    core = lax.axis_index("chan")
    pair = me // 2
    odd = me % 2
    mate = me + 1 - 2 * odd
    other = 1 - core
    has_low = pair > 0
    has_high = pair < seq_count // 2 - 1

    def rows_of(k):
        return pl.ds(pl.multiple_of(k * CHUNK, CHUNK), CHUNK)

    def piece_of(n):
        return pl.ds(pl.multiple_of(n * PIECE, PIECE), PIECE)

    def load(k):
        return (
            pltpu.make_async_copy(key_hbm.at[rows_of(k)], key.at[rows_of(k)], key_sem.at[k]),
            pltpu.make_async_copy(value_hbm.at[rows_of(k)], value.at[rows_of(k)], value_sem.at[k]),
        )

    def load_weight(k):
        return pltpu.make_async_copy(
            weight_hbm.at[rows_of(k)], weight.at[rows_of(k)], weight_sem.at[k]
        )

    load_query = pltpu.make_async_copy(query_hbm, query, query_sem)

    def far_copy(n):
        return pltpu.make_async_remote_copy(
            src_ref=product.at[piece_of(n)],
            dst_ref=back_two.at[piece_of(n)],
            send_sem=far_send.at[n],
            recv_sem=far_recv.at[n],
            device_id={"seq": me + 2},
            device_id_type=MESH,
        )

    def near_copy(n, source):
        return pltpu.make_async_remote_copy(
            src_ref=source.at[piece_of(n)],
            dst_ref=back_one.at[piece_of(n)],
            send_sem=near_send.at[n],
            recv_sem=near_recv.at[n],
            device_id={"seq": mate},
            device_id_type=MESH,
        )

    for k in range(chunks):
        for copy in load(k):
            copy.start()
    small = [
        pltpu.make_async_copy(source, target, small_sem.at[i])
        for i, (source, target) in enumerate(
            (
                (seed_hbm, seed_ref),
                (in_hbm, in_ref),
                (bias_hbm, bias_ref),
                (fout_hbm, fout_ref),
                (decay_hbm, decay_ref),
                (reach_hbm, reach_ref),
                (skip_hbm, skip_ref),
            )
        )
    ]
    for copy in small:
        copy.start()

    barrier = pltpu.get_barrier_semaphore()
    pl.semaphore_signal(barrier, inc=1, device_id={"seq": mate}, device_id_type=MESH)
    pl.semaphore_signal(barrier, inc=1, device_id={"chan": other}, device_id_type=MESH)

    @pl.when(has_low)
    def _():
        pl.semaphore_signal(barrier, inc=1, device_id={"seq": me - 2}, device_id_type=MESH)

    @pl.when(has_high)
    def _():
        pl.semaphore_signal(barrier, inc=1, device_id={"seq": me + 2}, device_id_type=MESH)

    def start_sends(n):
        @pl.when(has_high)
        def _():
            far_copy(n).start()

        @pl.when(odd == 0)
        def _():
            near_copy(n, product).start()

    for k in range(chunks):
        for copy in load(k):
            copy.wait()
        rows = slice(k * CHUNK, (k + 1) * CHUNK)
        part = key[rows].astype(jnp.float32) * value[rows].astype(jnp.float32)
        product[rows] = part.astype(jnp.bfloat16)
        if k == 0:
            pl.semaphore_wait(
                barrier, 2 + has_low.astype(jnp.int32) + has_high.astype(jnp.int32)
            )
        for n in range(k * CHUNK // PIECE, (k + 1) * CHUNK // PIECE):
            if n < AHEAD:
                start_sends(n)

    load_query.start()
    for k in range(chunks):
        load_weight(k).start()
    for copy in small:
        copy.wait()

    @pl.when(jnp.logical_not(has_low))
    def _():
        back_two[...] = jnp.zeros_like(back_two)

    @pl.when(me == 0)
    def _():
        back_one[...] = jnp.zeros_like(back_one)

    freqs = in_ref.shape[0] // 2
    hidden_count = in_ref.shape[1]
    lag = lax.broadcasted_iota(jnp.int32, (freqs, lags), 1)
    seeds = as_column(seed_ref[...].astype(jnp.float32), freqs).astype(jnp.int32)
    angles = ((seeds * lag) & (seq_len - 1)).astype(jnp.float32) * (2.0 * math.pi / seq_len)
    features = jnp.concatenate([jnp.cos(angles), jnp.sin(angles)], axis=0)
    first_dims = (((0,), (0,)), ((), ()))
    hidden = jnp.sin(
        lax.dot_general(
            in_ref[...],
            features,
            first_dims,
            precision=lax.Precision.HIGHEST,
            preferred_element_type=jnp.float32,
        )
        + as_column(bias_ref[...], hidden_count)
    )
    shaped = lax.dot_general(
        fout_ref[...],
        hidden,
        first_dims,
        precision=lax.Precision.HIGHEST,
        preferred_element_type=jnp.float32,
    )
    lag = lax.broadcasted_iota(jnp.int32, (filters, lags), 1).astype(jnp.float32)
    envelope = jnp.exp(-as_column(decay_ref[...], filters) * lag) * (1.0 / math.sqrt(lags))
    inside = lag < as_column(reach_ref[...].astype(jnp.float32), filters) * block
    taps[...] = (
        jnp.where(inside, shaped * envelope, 0.0).astype(jnp.bfloat16).astype(jnp.float32)
    )

    @pl.loop(0, channels // 128)
    def _(i):
        column = as_column(skip_ref[pl.ds(i, 1), :], 128)
        skip_wide[pl.ds(pl.multiple_of(i * 128, 128), 128), :] = jnp.broadcast_to(
            column, (128, block)
        )

    total[...] = jnp.zeros_like(total)
    load_query.wait()
    source_tok = lax.broadcasted_iota(jnp.int32, (block, block), 0)
    target_tok = lax.broadcasted_iota(jnp.int32, (block, block), 1)
    upper = target_tok >= source_tok

    def forward(n):
        far_copy(n).wait_recv()
        near_copy(n, back_two).start()

    relays = jnp.logical_and(has_low, odd == 1)

    @pl.when(relays)
    def _():
        forward(0)

    def step(n, half):
        more = n + AHEAD < pieces

        @pl.when(has_high)
        def _():
            far_copy(n).wait_send()

        @pl.when(odd == 0)
        def _():
            near_copy(n, product).wait_send()

        @pl.when(more)
        def _():
            start_sends(n + AHEAD)

        @pl.when(jnp.logical_and(relays, n + 1 < pieces))
        def _():
            forward(n + 1)

        @pl.when(jnp.logical_and(has_low, odd == 0))
        def _():
            far_copy(n).wait_recv()

        @pl.when(me > 0)
        def _():
            near_copy(n, product).wait_recv()

        for j in range(groups_piece):
            group = n * groups_piece + j
            rows = pl.ds(pl.multiple_of(group * per_group, per_group), per_group)
            tap_row = taps[pl.ds(group, 1), :]
            low = pltpu.roll(
                jnp.broadcast_to(tap_row[:, :block], (block, block)),
                0,
                1,
                stride=1,
                stride_axis=0,
            ).astype(jnp.bfloat16)
            high = pltpu.roll(
                jnp.broadcast_to(tap_row[:, block:], (block, block)),
                0,
                1,
                stride=1,
                stride_axis=0,
            ).astype(jnp.bfloat16)
            zero = jnp.zeros_like(low)
            toeplitz = jnp.concatenate(
                [
                    jnp.where(upper, zero, high),
                    jnp.where(upper, high, low),
                    jnp.where(upper, low, zero),
                ],
                axis=0,
            )
            own = product[rows, :]
            window = jnp.concatenate([back_two[rows, :], back_one[rows, :], own], axis=1)
            mixed = jnp.dot(window, toeplitz, preferred_element_type=jnp.float32)
            mixed = mixed + skip_wide[rows, :] * own.astype(jnp.float32)
            start = (half * groups_piece + j) * per_group
            gated[start : start + per_group, :] = (query[rows, :].astype(jnp.float32) * mixed).astype(jnp.bfloat16)

    @pl.loop(0, chunks)
    def _(k):
        for half in range(CHUNK // PIECE):
            step(k * (CHUNK // PIECE) + half, half)
        load_weight(k).wait()

        @pl.when(k < chunks - 1)
        def _():
            chunk = gated[...].T
            for half in range(2):
                total[half] += jnp.dot(
                    chunk,
                    weight[rows_of(k), half * cols : (half + 1) * cols],
                    preferred_element_type=jnp.float32,
                )

    chunk = gated[...].T
    last_rows = slice(channels - CHUNK, channels)

    def last(half, part):
        width = cols // PARTS
        columns = pl.ds(pl.multiple_of(half * cols + part * width, width), width)
        here = slice(part * width, (part + 1) * width)
        return total[half, :, here] + jnp.dot(
            chunk, weight[last_rows, columns], preferred_element_type=jnp.float32
        )

    def core_copy(part):
        return pltpu.make_async_remote_copy(
            src_ref=part_out.at[part],
            dst_ref=part_in.at[part],
            send_sem=core_send.at[part],
            recv_sem=core_recv.at[part],
            device_id={"chan": other},
            device_id_type=MESH,
        )

    for part in range(PARTS):
        part_out[part] = last(other, part).astype(jnp.bfloat16)
        core_copy(part).start()
    for part in range(PARTS):
        total[core, :, part * (cols // PARTS) : (part + 1) * (cols // PARTS)] = last(core, part)

    @pl.when(relays)
    def _():
        @pl.loop(0, pieces)
        def _(n):
            near_copy(n, back_two).wait_send()

    for part in range(PARTS):
        here = slice(part * (cols // PARTS), (part + 1) * (cols // PARTS))
        core_copy(part).wait()
        out_ref[:, here] = (total[core, :, here] + part_in[part].astype(jnp.float32)).astype(
            jnp.bfloat16
        )


def halo_body(
    query_feat,
    key_feat,
    value_feat,
    filter_seed,
    filter_in,
    filter_bias,
    filter_out,
    decay_rate,
    reach_blocks,
    skip_gain,
    out_weight,
):
    channels, block = query_feat.shape
    seq_count = lax.axis_size("seq")
    filters = decay_rate.shape[0]
    cols = out_weight.shape[1] // 2
    chunks = channels // CHUNK
    pieces = channels // PIECE
    small = (
        filter_seed.reshape(1, -1),
        filter_in,
        filter_bias.reshape(1, -1),
        filter_out,
        decay_rate.reshape(1, -1),
        reach_blocks.reshape(1, -1),
        skip_gain.reshape(-1, 128),
    )
    vmem = pl.BlockSpec(memory_space=pltpu.VMEM)
    anywhere = pl.BlockSpec(memory_space=pl.ANY)
    lags = block * 2
    stream = pltpu.VMEM((channels, block), jnp.bfloat16)
    return pl.pallas_call(
        functools.partial(halo_kernel, seq_count),
        out_shape=jax.ShapeDtypeStruct((block, cols), jnp.bfloat16),
        in_specs=[anywhere] * 11,
        out_specs=vmem,
        scratch_shapes=[
            *[pltpu.VMEM(array.shape, array.dtype) for array in small],
            stream,
            stream,
            stream,
            pltpu.VMEM(out_weight.shape, jnp.bfloat16),
            stream,
            stream,
            stream,
            pltpu.VMEM((filters, lags), jnp.float32),
            pltpu.VMEM((channels, block), jnp.float32),
            pltpu.VMEM((CHUNK, block), jnp.bfloat16),
            pltpu.VMEM((2, block, cols), jnp.float32),
            pltpu.VMEM((PARTS, block, cols // PARTS), jnp.bfloat16),
            pltpu.VMEM((PARTS, block, cols // PARTS), jnp.bfloat16),
            pltpu.SemaphoreType.DMA((len(small),)),
            pltpu.SemaphoreType.DMA((chunks,)),
            pltpu.SemaphoreType.DMA((chunks,)),
            pltpu.SemaphoreType.DMA,
            pltpu.SemaphoreType.DMA((chunks,)),
            pltpu.SemaphoreType.DMA((pieces,)),
            pltpu.SemaphoreType.DMA((pieces,)),
            pltpu.SemaphoreType.DMA((pieces,)),
            pltpu.SemaphoreType.DMA((pieces,)),
            pltpu.SemaphoreType.DMA((PARTS,)),
            pltpu.SemaphoreType.DMA((PARTS,)),
        ],
        compiler_params=pltpu.CompilerParams(
            collective_id=0, has_side_effects=True, vmem_limit_bytes=62 * 2**20
        ),
        name="halo_conv_project",
    )(
        query_feat,
        key_feat,
        value_feat,
        *small,
        out_weight,
    )


def filter_rows(
    lag_index,
    filter_seed,
    filter_in,
    filter_bias,
    filter_out,
    decay_rate,
    reach_blocks,
    block_len,
    seq_len,
    reach_max,
):
    safe_lag = jnp.maximum(lag_index, 0)
    phases = safe_lag[:, None] * filter_seed[None, :] % seq_len
    angles = phases.astype(jnp.float32) * (2.0 * math.pi / seq_len)
    features = jnp.concatenate([jnp.cos(angles), jnp.sin(angles)], axis=1)
    hidden = jnp.sin(
        jnp.dot(
            features, filter_in, precision=lax.Precision.HIGHEST, preferred_element_type=jnp.float32
        )
        + filter_bias
    )
    shaped = jnp.dot(
        hidden, filter_out, precision=lax.Precision.HIGHEST, preferred_element_type=jnp.float32
    )
    envelope = jnp.exp(-decay_rate[None, :] * safe_lag.astype(jnp.float32)[:, None]) * (
        1.0 / math.sqrt(reach_max * block_len)
    )
    inside = (lag_index[:, None] >= 0) & (lag_index[:, None] < reach_blocks[None, :] * block_len)
    return jnp.where(inside, shaped * envelope, 0.0).astype(jnp.bfloat16)


def hankel_rows(tap_rows, sub_len, span_len):
    return jnp.stack(
        [
            tap_rows[:, sub_len - 1 - offset : sub_len - 1 - offset + span_len]
            for offset in range(sub_len)
        ],
        axis=1,
    )


def body(
    query_feat,
    key_feat,
    value_feat,
    filter_seed,
    filter_in,
    filter_bias,
    filter_out,
    decay_rate,
    reach_blocks,
    skip_gain,
    out_weight,
):
    channels, block = query_feat.shape
    seq_count = lax.axis_size("seq")
    reach_max = seq_count // 4
    seq_len = block * seq_count
    sub_len = min(128, block)
    span_len = reach_max * block + sub_len
    rev_len = span_len + sub_len - 1
    filter_count = decay_rate.shape[0]
    per_group = channels // filter_count
    product = (key_feat.astype(jnp.float32) * value_feat.astype(jnp.float32)).astype(jnp.bfloat16)
    lag_index = reach_max * block + sub_len - 1 - lax.iota(jnp.int32, rev_len)
    taps = filter_rows(
        lag_index,
        filter_seed,
        filter_in,
        filter_bias,
        filter_out,
        decay_rate,
        reach_blocks,
        block,
        seq_len,
        reach_max,
    ).T
    seq_index = lax.axis_index("seq")
    spread, query_all = (
        lax.all_to_all(product, "seq", split_axis=0, concat_axis=1, tiled=True),
        lax.all_to_all(query_feat, "seq", split_axis=0, concat_axis=1, tiled=True),
    )
    chan_dev = spread.shape[0]
    full_len = spread.shape[1]
    padded = jnp.concatenate(
        [jnp.zeros((chan_dev, reach_max * block), jnp.bfloat16), spread], axis=1
    )
    pieces = padded.reshape(chan_dev, -1, sub_len)
    count_tiles = full_len // sub_len
    span_blocks = span_len // sub_len
    windows = jnp.concatenate([pieces[:, k : k + count_tiles] for k in range(span_blocks)], axis=2)
    first_chan = seq_index * chan_dev
    group_ids = (first_chan + lax.iota(jnp.int32, chan_dev)) // per_group
    chan_taps = jnp.take(taps, group_ids, axis=0)
    chan_block = math.gcd(8, chan_dev)
    windows = windows.reshape(chan_dev // chan_block, chan_block, count_tiles, span_len)
    chan_taps = chan_taps.reshape(chan_dev // chan_block, chan_block, rev_len)

    def convolve_chan(inputs_pair):
        window_part, tap_part = inputs_pair
        hankel = hankel_rows(tap_part, sub_len, span_len)
        return jnp.einsum("ctw,caw->cta", window_part, hankel, preferred_element_type=jnp.float32)

    convolved = lax.map(convolve_chan, (windows, chan_taps))
    convolved = convolved.reshape(chan_dev, full_len)
    skip_part = lax.dynamic_slice_in_dim(skip_gain, first_chan, chan_dev)
    mixed_part = convolved + skip_part[:, None] * spread.astype(jnp.float32)
    gated_part = (query_all.astype(jnp.float32) * mixed_part).astype(jnp.bfloat16)
    gated = lax.all_to_all(gated_part, "seq", split_axis=1, concat_axis=0, tiled=True)
    reduced = lax.psum_scatter(
        lax.dot_general(
            out_weight, gated, (((0,), (0,)), ((), ())), preferred_element_type=jnp.float32
        ),
        "chan",
        scatter_dimension=0,
        tiled=True,
    )
    return reduced.T.astype(jnp.bfloat16)


def solution(mesh):
    halo = mesh.shape["seq"] // 4 == 2 and mesh.shape["chan"] == 2
    return jax.shard_map(
        halo_body if halo else body,
        mesh=mesh,
        in_specs=(
            P("chan", ("groups", "seq")),
            P("chan", ("groups", "seq")),
            P("chan", ("groups", "seq")),
            P(),
            P(),
            P(),
            P(None, "chan"),
            P("chan"),
            P("chan"),
            P("chan"),
            P("chan", None),
        ),
        out_specs=P(("groups", "seq"), "chan"),
        check_vma=False,
    )
```

profile of v0, /device:TPU:17, one launch (start us, length us, event | category | flops | bytes accessed | tf_op | source)
XLA Modules:
  0.0 24.0 jit_solution(5827896211377530320)
XLA Ops:
  0.0 22.3 %halo_conv_project.1 = bf16[128,1024]{1,0:T(8,128)(2,1)} custom-call(bf16[2048,128]{1,0:T(8,128)(2,1)} %query_hbm.1, bf16[2048,128]{1,0:T(8,128)(2,1)} %key_hbm.1, bf16[2048,128]{1,0:T(8,128)(2,1)} %value_hbm.1, s32[1,16]{1,0:T(1,128)} %bitcast.6, f32[32,64]{1,0:T(8,128)} %in_hbm.1, f32[1,64]{1,0:T(1,128)} %bitcast.7, f32[64,128]{1,0:T(8,128)} %fout_hbm.1, ...), custom_call_target="tpu_custom_call" | custom-call | tf_op jit(solution)/shard_map/halo_conv_project/pallas_call | solution.py:402
  22.3 1.7 %copy.13 = bf16[128,1024]{1,0:T(8,128)(2,1)} copy(bf16[128,1024]{1,0:T(8,128)(2,1)} %halo_conv_project.1) | data formatting | bytes 524288
where the time goes:
time: 24.2 us; the launch traced here: 24 us
  Pallas kernels  22.3 us (92%)
  local copies, waits for them, and re-layouts  1.67 us (7%)
    pallas_call x1, Pallas kernels, halo_body(): pl.pallas_call(functools.partial(halo_kernel, seq_count), out_shape=jax.S...  22.3 us
    unnamed x1, local copies, waits for them, and re-layouts  1.67 us

commit v1 on v0

--- a/solution.py
+++ b/solution.py
@@ -10,8 +10,9 @@
 
 MESH = pl.DeviceIdType.MESH
 CHUNK = 256
-PIECE = 256
-AHEAD = 4
+PIECE = 128
+LAST = 64
+DIRECT = 0
 PARTS = 2
 
 
@@ -44,27 +45,23 @@
     reach_ref,
     skip_ref,
     query,
-    key,
-    value,
+    factors,
     weight,
     product,
-    back_two,
-    back_one,
+    back,
     taps,
+    toeplitz,
     skip_wide,
     gated,
     total,
     part_out,
     part_in,
     small_sem,
-    key_sem,
-    value_sem,
+    factor_sem,
     query_sem,
     weight_sem,
-    far_send,
-    far_recv,
-    near_send,
-    near_recv,
+    send_sem,
+    arrive_sem,
     core_send,
     core_recv,
 ):
@@ -73,10 +70,16 @@
     per_group = channels // filters
     lags = taps.shape[1]
     chunks = channels // CHUNK
-    pieces = channels // PIECE
+    halves = CHUNK // PIECE
     groups_piece = PIECE // per_group
     cols = out_ref.shape[1]
     seq_len = seq_count * block
+    whole = (channels - CHUNK) // PIECE
+    tail = piece_tail(channels)
+    pieces = whole + len(tail)
+    relayed = sum(n * PIECE < channels - DIRECT for n in range(whole)) + sum(
+        offset < channels - DIRECT for offset, _ in tail
+    )
 
     me = lax.axis_index("seq")
     core = lax.axis_index("chan")
@@ -86,49 +89,83 @@
     other = 1 - core
     has_low = pair > 0
     has_high = pair < seq_count // 2 - 1
+    even = odd == 0
+    relays = jnp.logical_and(has_low, odd == 1)
+    from_direct = jnp.logical_and(has_low, even)
+    to_direct = jnp.logical_and(has_high, odd == 1)
+
+    barrier = pltpu.get_barrier_semaphore()
+
+    def greet(device):
+        pl.semaphore_signal(barrier, inc=1, device_id=device, device_id_type=MESH)
+
+    greet({"chan": other})
+    pl.when(jnp.logical_or(odd == 1, has_low))(lambda: greet({"seq": mate}))
+    pl.when(has_low)(lambda: greet({"seq": me - 2}))
+    receivers = 1 + jnp.logical_or(even, has_low).astype(jnp.int32) + has_high.astype(jnp.int32)
+    if relayed < pieces:
+        pl.when(from_direct)(lambda: greet({"seq": me - 1}))
+        receivers = receivers + to_direct.astype(jnp.int32)
 
     def rows_of(k):
         return pl.ds(pl.multiple_of(k * CHUNK, CHUNK), CHUNK)
 
     def piece_of(n):
+        if isinstance(n, int) and n >= whole:
+            return pl.ds(*tail[n - whole])
         return pl.ds(pl.multiple_of(n * PIECE, PIECE), PIECE)
-
-    def load(k):
-        return (
-            pltpu.make_async_copy(key_hbm.at[rows_of(k)], key.at[rows_of(k)], key_sem.at[k]),
-            pltpu.make_async_copy(value_hbm.at[rows_of(k)], value.at[rows_of(k)], value_sem.at[k]),
-        )
 
     def load_weight(k):
         return pltpu.make_async_copy(
-            weight_hbm.at[rows_of(k)], weight.at[rows_of(k)], weight_sem.at[k]
-        )
-
+            weight_hbm.at[rows_of(k)], weight.at[rows_of(k)], weight_sem.at[k % 2]
+        )
+
+    load_key = pltpu.make_async_copy(key_hbm, factors.at[0], factor_sem)
+    load_value = pltpu.make_async_copy(value_hbm, factors.at[1], factor_sem)
     load_query = pltpu.make_async_copy(query_hbm, query, query_sem)
 
-    def far_copy(n):
+    def far_copy(rows, n):
         return pltpu.make_async_remote_copy(
-            src_ref=product.at[piece_of(n)],
-            dst_ref=back_two.at[piece_of(n)],
-            send_sem=far_send.at[n],
-            recv_sem=far_recv.at[n],
+            src_ref=product.at[rows],
+            dst_ref=back.at[0, rows],
+            send_sem=send_sem.at[0],
+            recv_sem=arrive_sem.at[n],
             device_id={"seq": me + 2},
             device_id_type=MESH,
         )
 
-    def near_copy(n, source):
+    def near_copy(rows, n):
         return pltpu.make_async_remote_copy(
-            src_ref=source.at[piece_of(n)],
-            dst_ref=back_one.at[piece_of(n)],
-            send_sem=near_send.at[n],
-            recv_sem=near_recv.at[n],
+            src_ref=product.at[rows],
+            dst_ref=back.at[1, rows],
+            send_sem=send_sem.at[1],
+            recv_sem=arrive_sem.at[n],
             device_id={"seq": mate},
             device_id_type=MESH,
         )
 
-    for k in range(chunks):
-        for copy in load(k):
-            copy.start()
+    def relay_copy(rows, n):
+        return pltpu.make_async_remote_copy(
+            src_ref=back.at[0, rows],
+            dst_ref=back.at[1, rows],
+            send_sem=send_sem.at[1],
+            recv_sem=arrive_sem.at[n],
+            device_id={"seq": mate},
+            device_id_type=MESH,
+        )
+
+    def direct_copy(rows, n):
+        return pltpu.make_async_remote_copy(
+            src_ref=product.at[rows],
+            dst_ref=back.at[1, rows],
+            send_sem=send_sem.at[2],
+            recv_sem=arrive_sem.at[n],
+            device_id={"seq": me + 1},
+            device_id_type=MESH,
+        )
+
+    load_key.start()
+    load_value.start()
     small = [
         pltpu.make_async_copy(source, target, small_sem.at[i])
         for i, (source, target) in enumerate(
@@ -146,54 +183,50 @@
     for copy in small:
         copy.start()
 
-    barrier = pltpu.get_barrier_semaphore()
-    pl.semaphore_signal(barrier, inc=1, device_id={"seq": mate}, device_id_type=MESH)
-    pl.semaphore_signal(barrier, inc=1, device_id={"chan": other}, device_id_type=MESH)
-
-    @pl.when(has_low)
-    def _():
-        pl.semaphore_signal(barrier, inc=1, device_id={"seq": me - 2}, device_id_type=MESH)
-
-    @pl.when(has_high)
-    def _():
-        pl.semaphore_signal(barrier, inc=1, device_id={"seq": me + 2}, device_id_type=MESH)
-
-    def start_sends(n):
+    def start_sends(first, last):
         @pl.when(has_high)
         def _():
-            far_copy(n).start()
-
-        @pl.when(odd == 0)
+            for n in range(first, min(last, relayed)):
+                far_copy(piece_of(n), n).start()
+
+        @pl.when(even)
         def _():
-            near_copy(n, product).start()
-
+            for n in range(first, last):
+                near_copy(piece_of(n), n).start()
+
+    pltpu.make_async_copy(factors, factors, factor_sem).wait()
     for k in range(chunks):
-        for copy in load(k):
-            copy.wait()
         rows = slice(k * CHUNK, (k + 1) * CHUNK)
-        part = key[rows].astype(jnp.float32) * value[rows].astype(jnp.float32)
+        part = factors[0, rows].astype(jnp.float32) * factors[1, rows].astype(jnp.float32)
         product[rows] = part.astype(jnp.bfloat16)
         if k == 0:
-            pl.semaphore_wait(
-                barrier, 2 + has_low.astype(jnp.int32) + has_high.astype(jnp.int32)
-            )
-        for n in range(k * CHUNK // PIECE, (k + 1) * CHUNK // PIECE):
-            if n < AHEAD:
-                start_sends(n)
+            pl.semaphore_wait(barrier, receivers)
+        start_sends(k * halves, (k + 1) * halves if k < chunks - 1 else pieces)
+
+    if relayed < pieces:
+
+        @pl.when(to_direct)
+        def _():
+            for n in range(relayed, pieces):
+                direct_copy(piece_of(n), n).start()
+
+        @pl.when(has_high)
+        def _():
+            for n in range(relayed, pieces):
+                far_copy(piece_of(n), n).start()
 
     load_query.start()
-    for k in range(chunks):
-        load_weight(k).start()
+    load_weight(0).start()
     for copy in small:
         copy.wait()
 
     @pl.when(jnp.logical_not(has_low))
     def _():
-        back_two[...] = jnp.zeros_like(back_two)
+        back[0] = jnp.zeros_like(back[0])
 
     @pl.when(me == 0)
     def _():
-        back_one[...] = jnp.zeros_like(back_one)
+        back[1] = jnp.zeros_like(back[1])
 
     freqs = in_ref.shape[0] // 2
     hidden_count = in_ref.shape[1]
@@ -226,105 +259,99 @@
         jnp.where(inside, shaped * envelope, 0.0).astype(jnp.bfloat16).astype(jnp.float32)
     )
 
-    @pl.loop(0, channels // 128)
-    def _(i):
-        column = as_column(skip_ref[pl.ds(i, 1), :], 128)
-        skip_wide[pl.ds(pl.multiple_of(i * 128, 128), 128), :] = jnp.broadcast_to(
-            column, (128, block)
-        )
-
     total[...] = jnp.zeros_like(total)
     load_query.wait()
     source_tok = lax.broadcasted_iota(jnp.int32, (block, block), 0)
     target_tok = lax.broadcasted_iota(jnp.int32, (block, block), 1)
     upper = target_tok >= source_tok
 
-    def forward(n):
-        far_copy(n).wait_recv()
-        near_copy(n, back_two).start()
-
-    relays = jnp.logical_and(has_low, odd == 1)
-
-    @pl.when(relays)
-    def _():
-        forward(0)
-
-    def step(n, half):
-        more = n + AHEAD < pieces
-
-        @pl.when(has_high)
+    def spread(row):
+        return pltpu.roll(
+            jnp.broadcast_to(row, (block, block)), 0, 1, stride=1, stride_axis=0
+        ).astype(jnp.bfloat16)
+
+    def band(group):
+        tap_row = taps[pl.ds(group, 1), :]
+        low = spread(tap_row[:, :block])
+        high = spread(tap_row[:, block:])
+        zero = jnp.zeros_like(low)
+        return (
+            jnp.where(upper, zero, high),
+            jnp.where(upper, high, low),
+            jnp.where(upper, low, zero),
+        )
+
+    def skip_rows(n):
+        return jnp.broadcast_to(skip_ref[pl.ds(n, 1), :], (PIECE, PIECE)).T
+
+    for n in range(halves):
+        skip_wide[n * PIECE : (n + 1) * PIECE, :] = skip_rows(whole + n)
+    for j in range(CHUNK // per_group):
+        for i, part in enumerate(band(whole * groups_piece + j)):
+            toeplitz[j, i * block : (i + 1) * block] = part
+
+    def arrive(n):
+        rows = piece_of(n)
+
+        @pl.when(has_low)
         def _():
-            far_copy(n).wait_send()
-
-        @pl.when(odd == 0)
+            both = back.at[:, rows]
+            pltpu.make_async_copy(both, both, arrive_sem.at[n]).wait()
+
+        @pl.when(me == 1)
         def _():
-            near_copy(n, product).wait_send()
-
-        @pl.when(more)
-        def _():
-            start_sends(n + AHEAD)
-
-        @pl.when(jnp.logical_and(relays, n + 1 < pieces))
-        def _():
-            forward(n + 1)
-
-        @pl.when(jnp.logical_and(has_low, odd == 0))
-        def _():
-            far_copy(n).wait_recv()
-
-        @pl.when(me > 0)
-        def _():
-            near_copy(n, product).wait_recv()
-
-        for j in range(groups_piece):
-            group = n * groups_piece + j
-            rows = pl.ds(pl.multiple_of(group * per_group, per_group), per_group)
-            tap_row = taps[pl.ds(group, 1), :]
-            low = pltpu.roll(
-                jnp.broadcast_to(tap_row[:, :block], (block, block)),
-                0,
-                1,
-                stride=1,
-                stride_axis=0,
-            ).astype(jnp.bfloat16)
-            high = pltpu.roll(
-                jnp.broadcast_to(tap_row[:, block:], (block, block)),
-                0,
-                1,
-                stride=1,
-                stride_axis=0,
-            ).astype(jnp.bfloat16)
-            zero = jnp.zeros_like(low)
-            toeplitz = jnp.concatenate(
-                [
-                    jnp.where(upper, zero, high),
-                    jnp.where(upper, high, low),
-                    jnp.where(upper, low, zero),
-                ],
-                axis=0,
+            near_copy(rows, n).wait_recv()
+
+        if isinstance(n, int):
+            if n < relayed:
+                pl.when(relays)(lambda: relay_copy(rows, n).start())
+        else:
+
+            @pl.when(jnp.logical_and(relays, n < relayed))
+            def _():
+                relay_copy(rows, n).start()
+
+    def gate(row, matrix, skip, place):
+        rows = pl.ds(pl.multiple_of(row, per_group), per_group)
+        own = product[rows, :]
+        window = jnp.concatenate([back[0, rows, :], back[1, rows, :], own], axis=1)
+        mixed = jnp.dot(window, matrix, preferred_element_type=jnp.float32)
+        mixed = mixed + skip * own.astype(jnp.float32)
+        gated[place : place + per_group, :] = (query[rows, :].astype(jnp.float32) * mixed).astype(
+            jnp.bfloat16
+        )
+
+    @pl.loop(0, chunks - 1)
+    def _(k):
+        load_weight(k + 1).start()
+        for half in range(halves):
+            n = k * halves + half
+            arrive(n)
+            skip = skip_rows(n)
+            for j in range(groups_piece):
+                start = j * per_group
+                matrix = jnp.concatenate(band(n * groups_piece + j), axis=0)
+                gate(
+                    n * PIECE + start,
+                    matrix,
+                    skip[start : start + per_group],
+                    half * PIECE + start,
+                )
+        load_weight(k).wait()
+        chunk = gated[...].T
+        for half in range(2):
+            total[half] += jnp.dot(
+                chunk,
+                weight[rows_of(k), half * cols : (half + 1) * cols],
+                preferred_element_type=jnp.float32,
             )
-            own = product[rows, :]
-            window = jnp.concatenate([back_two[rows, :], back_one[rows, :], own], axis=1)
-            mixed = jnp.dot(window, toeplitz, preferred_element_type=jnp.float32)
-            mixed = mixed + skip_wide[rows, :] * own.astype(jnp.float32)
-            start = (half * groups_piece + j) * per_group
-            gated[start : start + per_group, :] = (query[rows, :].astype(jnp.float32) * mixed).astype(jnp.bfloat16)
-
-    @pl.loop(0, chunks)
-    def _(k):
-        for half in range(CHUNK // PIECE):
-            step(k * (CHUNK // PIECE) + half, half)
-        load_weight(k).wait()
-
-        @pl.when(k < chunks - 1)
-        def _():
-            chunk = gated[...].T
-            for half in range(2):
-                total[half] += jnp.dot(
-                    chunk,
-                    weight[rows_of(k), half * cols : (half + 1) * cols],
-                    preferred_element_type=jnp.float32,
-                )
+
+    load_weight(chunks - 1).wait()
+    for i, (offset, size) in enumerate(tail):
+        arrive(whole + i)
+        for row in range(offset, offset + size, per_group):
+            place = row - (channels - CHUNK)
+            gate(row, toeplitz[place // per_group], skip_wide[place : place + per_group, :], place)
 
     chunk = gated[...].T
     last_rows = slice(channels - CHUNK, channels)
@@ -341,7 +368,7 @@
         return pltpu.make_async_remote_copy(
             src_ref=part_out.at[part],
             dst_ref=part_in.at[part],
-            send_sem=core_send.at[part],
+            send_sem=core_send,
             recv_sem=core_recv.at[part],
             device_id={"chan": other},
             device_id_type=MESH,
@@ -353,18 +380,39 @@
     for part in range(PARTS):
         total[core, :, part * (cols // PARTS) : (part + 1) * (cols // PARTS)] = last(core, part)
 
+    everything = slice(0, channels)
+
+    @pl.when(has_high)
+    def _():
+        far_copy(everything, 0).wait_send()
+
+    @pl.when(even)
+    def _():
+        near_copy(everything, 0).wait_send()
+
     @pl.when(relays)
     def _():
-        @pl.loop(0, pieces)
-        def _(n):
-            near_copy(n, back_two).wait_send()
-
+        relay_copy(slice(0, channels - DIRECT), 0).wait_send()
+
+    if relayed < pieces:
+
+        @pl.when(to_direct)
+        def _():
+            direct_copy(slice(channels - DIRECT, channels), 0).wait_send()
+
+    pltpu.make_async_copy(part_out, part_out, core_send).wait()
     for part in range(PARTS):
         here = slice(part * (cols // PARTS), (part + 1) * (cols // PARTS))
-        core_copy(part).wait()
+        core_copy(part).wait_recv()
         out_ref[:, here] = (total[core, :, here] + part_in[part].astype(jnp.float32)).astype(
             jnp.bfloat16
         )
+
+
+def piece_tail(channels):
+    start = channels - CHUNK
+    sizes = [PIECE] + [LAST] * ((CHUNK - PIECE) // LAST)
+    return [(start + sum(sizes[:i]), size) for i, size in enumerate(sizes)]
 
 
 def halo_body(
@@ -384,8 +432,7 @@
     seq_count = lax.axis_size("seq")
     filters = decay_rate.shape[0]
     cols = out_weight.shape[1] // 2
-    chunks = channels // CHUNK
-    pieces = channels // PIECE
+    pieces = (channels - CHUNK) // PIECE + len(piece_tail(channels))
     small = (
         filter_seed.reshape(1, -1),
         filter_in,
@@ -395,52 +442,44 @@
         reach_blocks.reshape(1, -1),
         skip_gain.reshape(-1, 128),
     )
-    vmem = pl.BlockSpec(memory_space=pltpu.VMEM)
-    anywhere = pl.BlockSpec(memory_space=pl.ANY)
     lags = block * 2
-    stream = pltpu.VMEM((channels, block), jnp.bfloat16)
     return pl.pallas_call(
         functools.partial(halo_kernel, seq_count),
-        out_shape=jax.ShapeDtypeStruct((block, cols), jnp.bfloat16),
-        in_specs=[anywhere] * 11,
-        out_specs=vmem,
+        out_shape=pltpu.VMEM((block, cols), jnp.bfloat16),
+        in_specs=[pl.BlockSpec(memory_space=pltpu.HBM)] * 11,
+        out_specs=pl.BlockSpec(memory_space=pltpu.VMEM),
         scratch_shapes=[
             *[pltpu.VMEM(array.shape, array.dtype) for array in small],
-            stream,
-            stream,
-            stream,
+            pltpu.VMEM((channels, block), jnp.bfloat16),
+            pltpu.VMEM((2, channels, block), jnp.bfloat16),
             pltpu.VMEM(out_weight.shape, jnp.bfloat16),
-            stream,
-            stream,
-            stream,
+            pltpu.VMEM((channels, block), jnp.bfloat16),
+            pltpu.VMEM((2, channels, block), jnp.bfloat16),
             pltpu.VMEM((filters, lags), jnp.float32),
-            pltpu.VMEM((channels, block), jnp.float32),
+            pltpu.VMEM((CHUNK * filters // channels, 3 * block, block), jnp.bfloat16),
+            pltpu.VMEM((CHUNK, block), jnp.float32),
             pltpu.VMEM((CHUNK, block), jnp.bfloat16),
             pltpu.VMEM((2, block, cols), jnp.float32),
             pltpu.VMEM((PARTS, block, cols // PARTS), jnp.bfloat16),
             pltpu.VMEM((PARTS, block, cols // PARTS), jnp.bfloat16),
             pltpu.SemaphoreType.DMA((len(small),)),
-            pltpu.SemaphoreType.DMA((chunks,)),
-            pltpu.SemaphoreType.DMA((chunks,)),
             pltpu.SemaphoreType.DMA,
-            pltpu.SemaphoreType.DMA((chunks,)),
+            pltpu.SemaphoreType.DMA,
+            pltpu.SemaphoreType.DMA((2,)),
+            pltpu.SemaphoreType.DMA((3,)),
             pltpu.SemaphoreType.DMA((pieces,)),
-            pltpu.SemaphoreType.DMA((pieces,)),
-            pltpu.SemaphoreType.DMA((pieces,)),
-            pltpu.SemaphoreType.DMA((pieces,)),
-            pltpu.SemaphoreType.DMA((PARTS,)),
+            pltpu.SemaphoreType.DMA,
             pltpu.SemaphoreType.DMA((PARTS,)),
         ],
         compiler_params=pltpu.CompilerParams(
-            collective_id=0, has_side_effects=True, vmem_limit_bytes=62 * 2**20
+            collective_id=0, has_side_effects=True, vmem_limit_bytes=32 * 2**20
         ),
         name="halo_conv_project",
     )(
-        query_feat,
-        key_feat,
-        value_feat,
-        *small,
-        out_weight,
+        *(
+            pltpu.with_memory_space_constraint(array, pltpu.HBM)
+            for array in (query_feat, key_feat, value_feat, *small, out_weight)
+        )
     )
 
 

time: 24.2 us -> 21.5 us (0.89)
  Pallas kernels: 22.3 us -> 20.6 us
  local copies, waits for them, and re-layouts: 1.67 us -> 0.71 us
    pallas_call x1, Pallas kernels: 22.3 us -> 20.6 us  [halo_body(): pl.pallas_call(functools.partial(halo_kernel, seq_count), out_shape=pltpu...]
    unnamed x1, local copies, waits for them, and re-layouts: 1.67 us -> 0.71 us
where the time goes in v1:
time: 21.5 us; the launch traced here: 21.4 us
  Pallas kernels  20.6 us (96%)
  local copies, waits for them, and re-layouts  0.71 us (3%)
    pallas_call x1, Pallas kernels, halo_body(): pl.pallas_call(functools.partial(halo_kernel, seq_count), out_shape=pltpu...  20.6 us
    unnamed x1, local copies, waits for them, and re-layouts  0.71 us

profile of v1, /device:TPU:17, one launch (start us, length us, event | category | flops | bytes accessed | tf_op | source)
XLA Modules:
  0.0 21.4 jit_solution(4790167072106857540)
XLA Ops:
  0.0 20.6 %halo_conv_project.1 = bf16[128,1024]{1,0:T(8,128)(2,1)S(1)} custom-call(bf16[2048,128]{1,0:T(8,128)(2,1)} %query_hbm.1, bf16[2048,128]{1,0:T(8,128)(2,1)} %key_hbm.1, bf16[2048,128]{1,0:T(8,128)(2,1)} %value_hbm.1, s32[1,16]{1,0:T(1,128)} %bitcast.6, f32[32,64]{1,0:T(8,128)} %in_hbm.1, f32[1,64]{1,0:T(1,128)} %bitcast.7, f32[64,128]{1,0:T(8,128)} %fout_hbm.1, ...), custom_call_target="tpu_custom_call" | custom-call | tf_op jit(solution)/shard_map/halo_conv_project/pallas_call | solution.py:446
  20.6 0.7 %copy.13 = bf16[128,1024]{1,0:T(8,128)(2,1)} copy(bf16[128,1024]{1,0:T(8,128)(2,1)S(1)} %halo_conv_project.1) | data formatting | bytes 524288

commit v2 on v1

--- a/solution.py
+++ b/solution.py
@@ -12,8 +12,7 @@
 CHUNK = 256
 PIECE = 128
 LAST = 64
-DIRECT = 0
-PARTS = 2
+EARLY = 8
 
 
 def as_column(row, size):
@@ -49,10 +48,13 @@
     weight,
     product,
     back,
+    lifted,
     taps,
     toeplitz,
     skip_wide,
     gated,
+    gated_tail,
+    weight_in,
     total,
     part_out,
     part_in,
@@ -62,6 +64,7 @@
     weight_sem,
     send_sem,
     arrive_sem,
+    lift_sem,
     core_send,
     core_recv,
 ):
@@ -77,9 +80,9 @@
     whole = (channels - CHUNK) // PIECE
     tail = piece_tail(channels)
     pieces = whole + len(tail)
-    relayed = sum(n * PIECE < channels - DIRECT for n in range(whole)) + sum(
-        offset < channels - DIRECT for offset, _ in tail
-    )
+    carried = list(range(whole - halves, whole))
+    carried_rows = slice(channels - 2 * CHUNK, channels - CHUNK)
+    order = [n for n in range(pieces) if n not in carried] + carried
 
     me = lax.axis_index("seq")
     core = lax.axis_index("chan")
@@ -91,8 +94,7 @@
     has_high = pair < seq_count // 2 - 1
     even = odd == 0
     relays = jnp.logical_and(has_low, odd == 1)
-    from_direct = jnp.logical_and(has_low, even)
-    to_direct = jnp.logical_and(has_high, odd == 1)
+    carries = jnp.logical_and(has_high, even)
 
     barrier = pltpu.get_barrier_semaphore()
 
@@ -100,12 +102,9 @@
         pl.semaphore_signal(barrier, inc=1, device_id=device, device_id_type=MESH)
 
     greet({"chan": other})
-    pl.when(jnp.logical_or(odd == 1, has_low))(lambda: greet({"seq": mate}))
+    greet({"seq": mate})
     pl.when(has_low)(lambda: greet({"seq": me - 2}))
-    receivers = 1 + jnp.logical_or(even, has_low).astype(jnp.int32) + has_high.astype(jnp.int32)
-    if relayed < pieces:
-        pl.when(from_direct)(lambda: greet({"seq": me - 1}))
-        receivers = receivers + to_direct.astype(jnp.int32)
+    receivers = 2 + has_high.astype(jnp.int32)
 
     def rows_of(k):
         return pl.ds(pl.multiple_of(k * CHUNK, CHUNK), CHUNK)
@@ -154,13 +153,55 @@
             device_id_type=MESH,
         )
 
-    def direct_copy(rows, n):
+    def lift_copy():
         return pltpu.make_async_remote_copy(
-            src_ref=product.at[rows],
-            dst_ref=back.at[1, rows],
+            src_ref=product.at[carried_rows],
+            dst_ref=lifted,
             send_sem=send_sem.at[2],
-            recv_sem=arrive_sem.at[n],
-            device_id={"seq": me + 1},
+            recv_sem=lift_sem,
+            device_id={"seq": mate},
+            device_id_type=MESH,
+        )
+
+    def carry_copy(i):
+        return pltpu.make_async_remote_copy(
+            src_ref=lifted.at[pl.ds(i * PIECE, PIECE)],
+            dst_ref=back.at[1, piece_of(carried[i])],
+            send_sem=send_sem.at[2],
+            recv_sem=arrive_sem.at[carried[i]],
+            device_id={"seq": me + 2},
+            device_id_type=MESH,
+        )
+
+    last_rows = slice(channels - CHUNK, channels)
+
+    def half_cols(half):
+        return pl.ds(pl.multiple_of(half * cols, cols), cols)
+
+    weight_copy = pltpu.make_async_remote_copy(
+        src_ref=weight_hbm.at[last_rows, half_cols(other)],
+        dst_ref=weight_in,
+        send_sem=core_send.at[0],
+        recv_sem=core_recv.at[0],
+        device_id={"chan": other},
+        device_id_type=MESH,
+    )
+    part_copy = pltpu.make_async_remote_copy(
+        src_ref=part_out,
+        dst_ref=part_in,
+        send_sem=core_send.at[1],
+        recv_sem=core_recv.at[1],
+        device_id={"chan": other},
+        device_id_type=MESH,
+    )
+
+    def gated_copy(rows, i):
+        return pltpu.make_async_remote_copy(
+            src_ref=gated_tail.at[0, rows],
+            dst_ref=gated_tail.at[1, rows],
+            send_sem=core_send.at[2],
+            recv_sem=core_recv.at[2 + i],
+            device_id={"chan": other},
             device_id_type=MESH,
         )
 
@@ -183,40 +224,55 @@
     for copy in small:
         copy.start()
 
-    def start_sends(first, last):
-        @pl.when(has_high)
-        def _():
-            for n in range(first, min(last, relayed)):
-                far_copy(piece_of(n), n).start()
-
-        @pl.when(even)
-        def _():
-            for n in range(first, last):
-                near_copy(piece_of(n), n).start()
-
     pltpu.make_async_copy(factors, factors, factor_sem).wait()
-    for k in range(chunks):
-        rows = slice(k * CHUNK, (k + 1) * CHUNK)
+
+    def multiply(rows):
         part = factors[0, rows].astype(jnp.float32) * factors[1, rows].astype(jnp.float32)
         product[rows] = part.astype(jnp.bfloat16)
-        if k == 0:
-            pl.semaphore_wait(barrier, receivers)
-        start_sends(k * halves, (k + 1) * halves if k < chunks - 1 else pieces)
-
-    if relayed < pieces:
-
-        @pl.when(to_direct)
-        def _():
-            for n in range(relayed, pieces):
-                direct_copy(piece_of(n), n).start()
-
-        @pl.when(has_high)
-        def _():
-            for n in range(relayed, pieces):
-                far_copy(piece_of(n), n).start()
+
+    def start_far(first, last):
+        for n in order[first:last]:
+            far_copy(piece_of(n), n).start()
+
+    def start_near(first, last):
+        for n in order[first:last]:
+            near_copy(piece_of(n), n).start()
+
+    half_rows = EARLY * PIECE
+    multiply(slice(0, half_rows))
+    multiply(carried_rows)
+    pl.semaphore_wait(barrier, receivers)
+
+    @pl.when(jnp.logical_and(odd == 1, has_high))
+    def _():
+        far_copy(piece_of(0), 0).start()
+        lift_copy().start()
+        start_far(1, EARLY)
+
+    @pl.when(carries)
+    def _():
+        for n in range(EARLY):
+            far_copy(piece_of(n), n).start()
+            near_copy(piece_of(n), n).start()
+
+    @pl.when(jnp.logical_and(even, jnp.logical_not(has_high)))
+    def _():
+        start_near(0, EARLY)
+
+    multiply(slice(half_rows, channels - 2 * CHUNK))
+    multiply(slice(channels - CHUNK, channels))
+
+    @pl.when(jnp.logical_and(odd == 1, has_high))
+    def _():
+        start_far(EARLY, pieces)
+
+    @pl.when(even)
+    def _():
+        start_near(EARLY, pieces)
 
     load_query.start()
     load_weight(0).start()
+    weight_copy.start()
     for copy in small:
         copy.wait()
 
@@ -290,40 +346,49 @@
         for i, part in enumerate(band(whole * groups_piece + j)):
             toeplitz[j, i * block : (i + 1) * block] = part
 
-    def arrive(n):
-        rows = piece_of(n)
-
-        @pl.when(has_low)
-        def _():
-            both = back.at[:, rows]
-            pltpu.make_async_copy(both, both, arrive_sem.at[n]).wait()
-
+    @pl.when(carries)
+    def _():
+        lift_copy().wait_recv()
+        for i in range(halves):
+            carry_copy(i).start()
+        for n in range(EARLY, pieces):
+            far_copy(piece_of(n), n).start()
+
+    def wait_both(n):
+        both = back.at[:, piece_of(n)]
+        pltpu.make_async_copy(both, both, arrive_sem.at[n]).wait()
+
+    def wait_first(n):
         @pl.when(me == 1)
         def _():
-            near_copy(rows, n).wait_recv()
-
-        if isinstance(n, int):
-            if n < relayed:
-                pl.when(relays)(lambda: relay_copy(rows, n).start())
-        else:
-
-            @pl.when(jnp.logical_and(relays, n < relayed))
-            def _():
-                relay_copy(rows, n).start()
-
-    def gate(row, matrix, skip, place):
+            near_copy(piece_of(n), n).wait_recv()
+
+    def arrive(n):
+        pl.when(has_low)(lambda: wait_both(n))
+        wait_first(n)
+
+        @pl.when(jnp.logical_and(relays, n < carried[0]))
+        def _():
+            relay_copy(piece_of(n), n).start()
+
+    def gate(row, matrix, skip):
         rows = pl.ds(pl.multiple_of(row, per_group), per_group)
         own = product[rows, :]
         window = jnp.concatenate([back[0, rows, :], back[1, rows, :], own], axis=1)
         mixed = jnp.dot(window, matrix, preferred_element_type=jnp.float32)
         mixed = mixed + skip * own.astype(jnp.float32)
-        gated[place : place + per_group, :] = (query[rows, :].astype(jnp.float32) * mixed).astype(
-            jnp.bfloat16
-        )
+        return (query[rows, :].astype(jnp.float32) * mixed).astype(jnp.bfloat16)
 
     @pl.loop(0, chunks - 1)
     def _(k):
         load_weight(k + 1).start()
+
+        @pl.when(jnp.logical_and(relays, k == chunks - 2))
+        def _():
+            for n in range(whole, pieces):
+                wait_both(n)
+                relay_copy(piece_of(n), n).start()
+
         for half in range(halves):
             n = k * halves + half
             arrive(n)
@@ -331,11 +396,9 @@
             for j in range(groups_piece):
                 start = j * per_group
                 matrix = jnp.concatenate(band(n * groups_piece + j), axis=0)
-                gate(
-                    n * PIECE + start,
-                    matrix,
-                    skip[start : start + per_group],
-                    half * PIECE + start,
+                place = half * PIECE + start
+                gated[place : place + per_group, :] = gate(
+                    n * PIECE + start, matrix, skip[start : start + per_group]
                 )
         load_weight(k).wait()
         chunk = gated[...].T
@@ -346,39 +409,31 @@
                 preferred_element_type=jnp.float32,
             )
 
+    part_out[...] = total[other].astype(jnp.bfloat16)
+    part_copy.start()
     load_weight(chunks - 1).wait()
     for i, (offset, size) in enumerate(tail):
-        arrive(whole + i)
+        pl.when(jnp.logical_and(has_low, even))(lambda: wait_both(whole + i))
+        wait_first(whole + i)
         for row in range(offset, offset + size, per_group):
             place = row - (channels - CHUNK)
-            gate(row, toeplitz[place // per_group], skip_wide[place : place + per_group, :], place)
-
-    chunk = gated[...].T
-    last_rows = slice(channels - CHUNK, channels)
-
-    def last(half, part):
-        width = cols // PARTS
-        columns = pl.ds(pl.multiple_of(half * cols + part * width, width), width)
-        here = slice(part * width, (part + 1) * width)
-        return total[half, :, here] + jnp.dot(
-            chunk, weight[last_rows, columns], preferred_element_type=jnp.float32
-        )
-
-    def core_copy(part):
-        return pltpu.make_async_remote_copy(
-            src_ref=part_out.at[part],
-            dst_ref=part_in.at[part],
-            send_sem=core_send,
-            recv_sem=core_recv.at[part],
-            device_id={"chan": other},
-            device_id_type=MESH,
-        )
-
-    for part in range(PARTS):
-        part_out[part] = last(other, part).astype(jnp.bfloat16)
-        core_copy(part).start()
-    for part in range(PARTS):
-        total[core, :, part * (cols // PARTS) : (part + 1) * (cols // PARTS)] = last(core, part)
+            gated_tail[0, place : place + per_group, :] = gate(
+                row, toeplitz[place // per_group], skip_wide[place : place + per_group, :]
+            )
+        place = offset - (channels - CHUNK)
+        gated_copy(slice(place, place + size), min(i, 1)).start()
+
+    part_copy.wait_recv()
+    total[core] += part_in[...].astype(jnp.float32) + jnp.dot(
+        gated_tail[0].T, weight[last_rows, half_cols(core)], preferred_element_type=jnp.float32
+    )
+    weight_copy.wait_recv()
+    first_tail = slice(0, tail[0][1])
+    rest_tail = slice(tail[0][1], CHUNK)
+    gated_copy(first_tail, 0).wait_recv()
+    total[core] += jnp.dot(
+        gated_tail[1, first_tail].T, weight_in[first_tail], preferred_element_type=jnp.float32
+    )
 
     everything = slice(0, channels)
 
@@ -392,21 +447,20 @@
 
     @pl.when(relays)
     def _():
-        relay_copy(slice(0, channels - DIRECT), 0).wait_send()
-
-    if relayed < pieces:
-
-        @pl.when(to_direct)
-        def _():
-            direct_copy(slice(channels - DIRECT, channels), 0).wait_send()
-
-    pltpu.make_async_copy(part_out, part_out, core_send).wait()
-    for part in range(PARTS):
-        here = slice(part * (cols // PARTS), (part + 1) * (cols // PARTS))
-        core_copy(part).wait_recv()
-        out_ref[:, here] = (total[core, :, here] + part_in[part].astype(jnp.float32)).astype(
-            jnp.bfloat16
-        )
+        relay_copy(slice(0, channels - CHUNK), 0).wait_send()
+
+    @pl.when(has_high)
+    def _():
+        lift_copy().wait_send()
+
+    weight_copy.wait_send()
+    part_copy.wait_send()
+    gated_copy(slice(0, CHUNK), 0).wait_send()
+    gated_copy(rest_tail, 1).wait_recv()
+    out_ref[...] = (
+        total[core]
+        + jnp.dot(gated_tail[1, rest_tail].T, weight_in[rest_tail], preferred_element_type=jnp.float32)
+    ).astype(jnp.bfloat16)
 
 
 def piece_tail(channels):
@@ -455,13 +509,16 @@
             pltpu.VMEM(out_weight.shape, jnp.bfloat16),
             pltpu.VMEM((channels, block), jnp.bfloat16),
             pltpu.VMEM((2, channels, block), jnp.bfloat16),
+            pltpu.VMEM((CHUNK, block), jnp.bfloat16),
             pltpu.VMEM((filters, lags), jnp.float32),
             pltpu.VMEM((CHUNK * filters // channels, 3 * block, block), jnp.bfloat16),
             pltpu.VMEM((CHUNK, block), jnp.float32),
             pltpu.VMEM((CHUNK, block), jnp.bfloat16),
+            pltpu.VMEM((2, CHUNK, block), jnp.bfloat16),
+            pltpu.VMEM((CHUNK, cols), jnp.bfloat16),
             pltpu.VMEM((2, block, cols), jnp.float32),
-            pltpu.VMEM((PARTS, block, cols // PARTS), jnp.bfloat16),
-            pltpu.VMEM((PARTS, block, cols // PARTS), jnp.bfloat16),
+            pltpu.VMEM((block, cols), jnp.bfloat16),
+            pltpu.VMEM((block, cols), jnp.bfloat16),
             pltpu.SemaphoreType.DMA((len(small),)),
             pltpu.SemaphoreType.DMA,
             pltpu.SemaphoreType.DMA,
@@ -469,7 +526,8 @@
             pltpu.SemaphoreType.DMA((3,)),
             pltpu.SemaphoreType.DMA((pieces,)),
             pltpu.SemaphoreType.DMA,
-            pltpu.SemaphoreType.DMA((PARTS,)),
+            pltpu.SemaphoreType.DMA((3,)),
+            pltpu.SemaphoreType.DMA((4,)),
         ],
         compiler_params=pltpu.CompilerParams(
             collective_id=0, has_side_effects=True, vmem_limit_bytes=32 * 2**20

time: 21.5 us -> 21 us (0.977)
  Pallas kernels: 20.6 us -> 20.1 us
    pallas_call x1, Pallas kernels: 20.6 us -> 20.1 us  [halo_body(): pl.pallas_call(functools.partial(halo_kernel, seq_count), out_shape=pltpu...]
where the time goes in v2:
time: 21 us; the launch traced here: 20.8 us
  Pallas kernels  20.1 us (96%)
  local copies, waits for them, and re-layouts  0.71 us (3%)
    pallas_call x1, Pallas kernels, halo_body(): pl.pallas_call(functools.partial(halo_kernel, seq_count), out_shape=pltpu...  20.1 us
    unnamed x1, local copies, waits for them, and re-layouts  0.71 us

profile of v2, /device:TPU:17, one launch (start us, length us, event | category | flops | bytes accessed | tf_op | source)
XLA Modules:
  0.0 20.8 jit_solution(10075452553913386782)
XLA Ops:
  0.0 20.1 %halo_conv_project.1 = bf16[128,1024]{1,0:T(8,128)(2,1)S(1)} custom-call(bf16[2048,128]{1,0:T(8,128)(2,1)} %query_hbm.1, bf16[2048,128]{1,0:T(8,128)(2,1)} %key_hbm.1, bf16[2048,128]{1,0:T(8,128)(2,1)} %value_hbm.1, s32[1,16]{1,0:T(1,128)} %bitcast.6, f32[32,64]{1,0:T(8,128)} %in_hbm.1, f32[1,64]{1,0:T(1,128)} %bitcast.7, f32[64,128]{1,0:T(8,128)} %fout_hbm.1, ...), custom_call_target="tpu_custom_call" | custom-call | tf_op jit(solution)/shard_map/halo_conv_project/pallas_call | solution.py:500
  20.1 0.7 %copy.13 = bf16[128,1024]{1,0:T(8,128)(2,1)} copy(bf16[128,1024]{1,0:T(8,128)(2,1)S(1)} %halo_conv_project.1) | data formatting | bytes 524288

commit v3 on v2

--- a/solution.py
+++ b/solution.py
@@ -13,6 +13,7 @@
 PIECE = 128
 LAST = 64
 EARLY = 8
+READY = 3
 
 
 def as_column(row, size):
@@ -342,9 +343,15 @@
 
     for n in range(halves):
         skip_wide[n * PIECE : (n + 1) * PIECE, :] = skip_rows(whole + n)
+    first_ready = READY * CHUNK // per_group
+    tail_ready = (channels - CHUNK) // per_group - first_ready
+
+    def make_ready(slot):
+        for i, part in enumerate(band(first_ready + slot)):
+            toeplitz[slot, i * block : (i + 1) * block] = part
+
     for j in range(CHUNK // per_group):
-        for i, part in enumerate(band(whole * groups_piece + j)):
-            toeplitz[j, i * block : (i + 1) * block] = part
+        make_ready(tail_ready + j)
 
     @pl.when(carries)
     def _():
@@ -353,6 +360,13 @@
             carry_copy(i).start()
         for n in range(EARLY, pieces):
             far_copy(piece_of(n), n).start()
+
+    @pl.when(even)
+    def _():
+        @pl.loop(0, tail_ready // groups_piece)
+        def _(i):
+            for j in range(groups_piece):
+                make_ready(i * groups_piece + j)
 
     def wait_both(n):
         both = back.at[:, piece_of(n)]
@@ -392,14 +406,27 @@
         for half in range(halves):
             n = k * halves + half
             arrive(n)
-            skip = skip_rows(n)
-            for j in range(groups_piece):
-                start = j * per_group
-                matrix = jnp.concatenate(band(n * groups_piece + j), axis=0)
-                place = half * PIECE + start
-                gated[place : place + per_group, :] = gate(
-                    n * PIECE + start, matrix, skip[start : start + per_group]
-                )
+            ready = jnp.logical_and(even, k >= READY)
+
+            def convolve(matrix_of):
+                skip = skip_rows(n)
+                for j in range(groups_piece):
+                    start = j * per_group
+                    place = half * PIECE + start
+                    gated[place : place + per_group, :] = gate(
+                        n * PIECE + start,
+                        matrix_of(n * groups_piece + j),
+                        skip[start : start + per_group],
+                    )
+
+            @pl.when(ready)
+            def _():
+                convolve(lambda group: toeplitz[group - first_ready])
+
+            @pl.when(jnp.logical_not(ready))
+            def _():
+                convolve(lambda group: jnp.concatenate(band(group), axis=0))
+
         load_weight(k).wait()
         chunk = gated[...].T
         for half in range(2):
@@ -418,7 +445,7 @@
         for row in range(offset, offset + size, per_group):
             place = row - (channels - CHUNK)
             gated_tail[0, place : place + per_group, :] = gate(
-                row, toeplitz[place // per_group], skip_wide[place : place + per_group, :]
+                row, toeplitz[tail_ready + place // per_group], skip_wide[place : place + per_group, :]
             )
         place = offset - (channels - CHUNK)
         gated_copy(slice(place, place + size), min(i, 1)).start()
@@ -511,7 +538,9 @@
             pltpu.VMEM((2, channels, block), jnp.bfloat16),
             pltpu.VMEM((CHUNK, block), jnp.bfloat16),
             pltpu.VMEM((filters, lags), jnp.float32),
-            pltpu.VMEM((CHUNK * filters // channels, 3 * block, block), jnp.bfloat16),
+            pltpu.VMEM(
+                ((channels - READY * CHUNK) * filters // channels, 3 * block, block), jnp.bfloat16
+            ),
             pltpu.VMEM((CHUNK, block), jnp.float32),
             pltpu.VMEM((CHUNK, block), jnp.bfloat16),
             pltpu.VMEM((2, CHUNK, block), jnp.bfloat16),

time: 21 us -> 20.8 us (level)
    pallas_call x1, Pallas kernels: 20.1 us -> 19.9 us  [halo_body(): pl.pallas_call(functools.partial(halo_kernel, seq_count), out_shape=pltpu...]
where the time goes in v3:
time: 20.8 us; the launch traced here: 20.6 us
  Pallas kernels  19.9 us (96%)
  local copies, waits for them, and re-layouts  0.71 us (3%)
    pallas_call x1, Pallas kernels, halo_body(): pl.pallas_call(functools.partial(halo_kernel, seq_count), out_shape=pltpu...  19.9 us
    unnamed x1, local copies, waits for them, and re-layouts  0.71 us

profile of v3, /device:TPU:17, one launch (start us, length us, event | category | flops | bytes accessed | tf_op | source)
XLA Modules:
  0.0 20.6 jit_solution(3380362549205544823)
XLA Ops:
  0.0 19.9 %halo_conv_project.1 = bf16[128,1024]{1,0:T(8,128)(2,1)S(1)} custom-call(bf16[2048,128]{1,0:T(8,128)(2,1)} %query_hbm.1, bf16[2048,128]{1,0:T(8,128)(2,1)} %key_hbm.1, bf16[2048,128]{1,0:T(8,128)(2,1)} %value_hbm.1, s32[1,16]{1,0:T(1,128)} %bitcast.6, f32[32,64]{1,0:T(8,128)} %in_hbm.1, f32[1,64]{1,0:T(1,128)} %bitcast.7, f32[64,128]{1,0:T(8,128)} %fout_hbm.1, ...), custom_call_target="tpu_custom_call" | custom-call | tf_op jit(solution)/shard_map/halo_conv_project/pallas_call | solution.py:527
  19.9 0.7 %copy.13 = bf16[128,1024]{1,0:T(8,128)(2,1)} copy(bf16[128,1024]{1,0:T(8,128)(2,1)S(1)} %halo_conv_project.1) | data formatting | bytes 524288

commit v4 on v3

--- a/solution.py
+++ b/solution.py
@@ -12,8 +12,9 @@
 CHUNK = 256
 PIECE = 128
 LAST = 64
-EARLY = 8
-READY = 3
+EARLY = 6
+READY = 4
+CARRY_AT = 5
 
 
 def as_column(row, size):
@@ -115,10 +116,14 @@
             return pl.ds(*tail[n - whole])
         return pl.ds(pl.multiple_of(n * PIECE, PIECE), PIECE)
 
+    def chunk_at(k):
+        lifted_chunk = chunks - 2
+        moved = jnp.where(k == CARRY_AT, lifted_chunk, jnp.where(k > CARRY_AT, k - 1, k))
+        return jnp.where(jnp.logical_and(even, k <= lifted_chunk), moved, k)
+
     def load_weight(k):
-        return pltpu.make_async_copy(
-            weight_hbm.at[rows_of(k)], weight.at[rows_of(k)], weight_sem.at[k % 2]
-        )
+        rows = rows_of(chunk_at(k))
+        return pltpu.make_async_copy(weight_hbm.at[rows], weight.at[rows], weight_sem.at[k % 2])
 
     load_key = pltpu.make_async_copy(key_hbm, factors.at[0], factor_sem)
     load_value = pltpu.make_async_copy(value_hbm, factors.at[1], factor_sem)
@@ -377,13 +382,16 @@
         def _():
             near_copy(piece_of(n), n).wait_recv()
 
-    def arrive(n):
-        pl.when(has_low)(lambda: wait_both(n))
+    def relay(n):
+        wait_both(n)
+        relay_copy(piece_of(n), n).start()
+
+    def arrive(n, first):
+        ahead = jnp.logical_and(relays, n < carried[0])
+        pl.when(jnp.logical_and(has_low, jnp.logical_not(ahead)))(lambda: wait_both(n))
         wait_first(n)
-
-        @pl.when(jnp.logical_and(relays, n < carried[0]))
-        def _():
-            relay_copy(piece_of(n), n).start()
+        if not first:
+            pl.when(ahead)(lambda: relay(n))
 
     def gate(row, matrix, skip):
         rows = pl.ds(pl.multiple_of(row, per_group), per_group)
@@ -393,19 +401,15 @@
         mixed = mixed + skip * own.astype(jnp.float32)
         return (query[rows, :].astype(jnp.float32) * mixed).astype(jnp.bfloat16)
 
+    pl.when(relays)(lambda: relay(0))
+
     @pl.loop(0, chunks - 1)
     def _(k):
         load_weight(k + 1).start()
 
-        @pl.when(jnp.logical_and(relays, k == chunks - 2))
-        def _():
-            for n in range(whole, pieces):
-                wait_both(n)
-                relay_copy(piece_of(n), n).start()
-
         for half in range(halves):
-            n = k * halves + half
-            arrive(n)
+            n = chunk_at(k) * halves + half
+            arrive(n, half == 0)
             ready = jnp.logical_and(even, k >= READY)
 
             def convolve(matrix_of):
@@ -427,12 +431,21 @@
             def _():
                 convolve(lambda group: jnp.concatenate(band(group), axis=0))
 
+        @pl.when(jnp.logical_and(relays, k < chunks - 3))
+        def _():
+            relay((k + 1) * halves)
+
+        @pl.when(jnp.logical_and(relays, k == chunks - 3))
+        def _():
+            for n in range(whole, pieces):
+                relay(n)
+
         load_weight(k).wait()
         chunk = gated[...].T
         for half in range(2):
             total[half] += jnp.dot(
                 chunk,
-                weight[rows_of(k), half * cols : (half + 1) * cols],
+                weight[rows_of(chunk_at(k)), half * cols : (half + 1) * cols],
                 preferred_element_type=jnp.float32,
             )
 
@@ -450,8 +463,7 @@
         place = offset - (channels - CHUNK)
         gated_copy(slice(place, place + size), min(i, 1)).start()
 
-    part_copy.wait_recv()
-    total[core] += part_in[...].astype(jnp.float32) + jnp.dot(
+    total[core] += jnp.dot(
         gated_tail[0].T, weight[last_rows, half_cols(core)], preferred_element_type=jnp.float32
     )
     weight_copy.wait_recv()
@@ -483,9 +495,11 @@
     weight_copy.wait_send()
     part_copy.wait_send()
     gated_copy(slice(0, CHUNK), 0).wait_send()
+    part_copy.wait_recv()
     gated_copy(rest_tail, 1).wait_recv()
     out_ref[...] = (
         total[core]
+        + part_in[...].astype(jnp.float32)
         + jnp.dot(gated_tail[1, rest_tail].T, weight_in[rest_tail], preferred_element_type=jnp.float32)
     ).astype(jnp.bfloat16)
 

time: 20.8 us -> 20.7 us (level)
  no operation moved by 1% of the time
where the time goes in v4:
time: 20.7 us; the launch traced here: 20.5 us
  Pallas kernels  19.8 us (96%)
  local copies, waits for them, and re-layouts  0.71 us (3%)
    pallas_call x1, Pallas kernels, halo_body(): pl.pallas_call(functools.partial(halo_kernel, seq_count), out_shape=pltpu...  19.8 us
    unnamed x1, local copies, waits for them, and re-layouts  0.71 us

profile of v4, /device:TPU:17, one launch (start us, length us, event | category | flops | bytes accessed | tf_op | source)
XLA Modules:
  0.0 20.5 jit_solution(4113557549022732079)
XLA Ops:
  0.0 19.8 %halo_conv_project.1 = bf16[128,1024]{1,0:T(8,128)(2,1)S(1)} custom-call(bf16[2048,128]{1,0:T(8,128)(2,1)} %query_hbm.1, bf16[2048,128]{1,0:T(8,128)(2,1)} %key_hbm.1, bf16[2048,128]{1,0:T(8,128)(2,1)} %value_hbm.1, s32[1,16]{1,0:T(1,128)} %bitcast.6, f32[32,64]{1,0:T(8,128)} %in_hbm.1, f32[1,64]{1,0:T(1,128)} %bitcast.7, f32[64,128]{1,0:T(8,128)} %fout_hbm.1, ...), custom_call_target="tpu_custom_call" | custom-call | tf_op jit(solution)/shard_map/halo_conv_project/pallas_call | solution.py:541
  19.8 0.7 %copy.13 = bf16[128,1024]{1,0:T(8,128)(2,1)} copy(bf16[128,1024]{1,0:T(8,128)(2,1)S(1)} %halo_conv_project.1) | data formatting | bytes 524288

commit v5 on v4

--- a/solution.py
+++ b/solution.py
@@ -11,7 +11,7 @@
 MESH = pl.DeviceIdType.MESH
 CHUNK = 256
 PIECE = 128
-LAST = 64
+LAST = 128
 EARLY = 6
 READY = 4
 CARRY_AT = 5

time: 20.7 us -> 20.4 us (0.986)
  Pallas kernels: 19.8 us -> 19.5 us
    pallas_call x1, Pallas kernels: 19.8 us -> 19.5 us  [halo_body(): pl.pallas_call(functools.partial(halo_kernel, seq_count), out_shape=pltpu...]
where the time goes in v5:
time: 20.4 us; the launch traced here: 20.2 us
  Pallas kernels  19.5 us (96%)
  local copies, waits for them, and re-layouts  0.71 us (3%)
    pallas_call x1, Pallas kernels, halo_body(): pl.pallas_call(functools.partial(halo_kernel, seq_count), out_shape=pltpu...  19.5 us
    unnamed x1, local copies, waits for them, and re-layouts  0.71 us

profile of v5, /device:TPU:17, one launch (start us, length us, event | category | flops | bytes accessed | tf_op | source)
XLA Modules:
  0.0 20.2 jit_solution(1839174643913181791)
XLA Ops:
  0.0 19.5 %halo_conv_project.1 = bf16[128,1024]{1,0:T(8,128)(2,1)S(1)} custom-call(bf16[2048,128]{1,0:T(8,128)(2,1)} %query_hbm.1, bf16[2048,128]{1,0:T(8,128)(2,1)} %key_hbm.1, bf16[2048,128]{1,0:T(8,128)(2,1)} %value_hbm.1, s32[1,16]{1,0:T(1,128)} %bitcast.6, f32[32,64]{1,0:T(8,128)} %in_hbm.1, f32[1,64]{1,0:T(1,128)} %bitcast.7, f32[64,128]{1,0:T(8,128)} %fout_hbm.1, ...), custom_call_target="tpu_custom_call" | custom-call | tf_op jit(solution)/shard_map/halo_conv_project/pallas_call | solution.py:541
  19.5 0.7 %copy.13 = bf16[128,1024]{1,0:T(8,128)(2,1)} copy(bf16[128,1024]{1,0:T(8,128)(2,1)S(1)} %halo_conv_project.1) | data formatting | bytes 524288
